TPU v7x, 256 devices: a whole 4x4x8 slice. The times are simulated.
256 devices in a mesh: dp: 4 (over x), expert: 64 (over z, y, core).
Axes of the slice: x: 4, y: 4, z: 8, core: 2. Of those that a mesh axis runs over, the one named last changes fastest.
Arguments:
- tokens: bfloat16 [32768, 4096], P(('dp', 'expert')), may hold values from -6 to 6
- grad_out: bfloat16 [32768, 4096], P(('dp', 'expert')), may hold values from -2 to 2
- gate_prob: float32 [32768], P(('dp', 'expert')), may hold values from 0.1 to 1
- expert_ids: int32 [32768, 1], P(('dp', 'expert')), may hold values from 0 to 63; in each aligned block of 128 rows (0 to 127, 128 to 255, ...) at most 3 rows name the same one
- w_in: bfloat16 [64, 4096, 1024], P('expert', 'dp'), may hold values from -0.09375 to 0.09375
- w_out: bfloat16 [64, 4096, 1024], P('expert', 'dp'), may hold values from -0.1875 to 0.1875
- threshold: float32 [64, 1024], P('expert'), may hold values from 0.25 to 1
- spike_counts: int32 [64, 768, 1024], P('expert', 'dp'), may hold values from 0 to 4
Outputs:
- token_grad: bfloat16 [32768, 4096], P(('dp', 'expert'))
- w_in_grad: bfloat16 [64, 4096, 1024], P('expert', 'dp')
- w_out_grad: bfloat16 [64, 4096, 1024], P('expert', 'dp')
Inputs may be any that keep to these rules, and one draw needn't show every extreme that they name: `expert_ids`: in each device's block of 128 tokens no expert is chosen by more than 3 tokens, and some expert is chosen by exactly 3.
All inputs are finite; a program needn't handle non-finite values.
Results may differ from a plain program's by a relative error of at most 0.0057.
Values may be sent and summed in bfloat16 or wider, within the bound.
A program may use at most 128 MiB of HBM per device.

v0:
```python
import jax
import jax.numpy as jnp
from jax import lax
from jax.sharding import PartitionSpec as P

STEPS = 4


sharpness = 4.0


def selection(block_ids, expert_count, capacity):
    onehot = (block_ids[:, None] == jnp.arange(expert_count, dtype=jnp.int32)[None, :]).astype(
        jnp.int32
    )
    before = jnp.cumsum(onehot, axis=0) - onehot
    slot = jnp.sum(onehot * before, axis=1)
    place = block_ids * capacity + slot
    targets = jnp.arange(expert_count * capacity, dtype=jnp.int32)
    return (targets[:, None] == place[None, :]).astype(jnp.bfloat16)


def surrogate(membrane, limit):
    total = jnp.zeros_like(membrane)
    for step in range(STEPS):
        shifted = sharpness * (membrane - (step + 0.5) * limit[None, :])
        sig = jax.nn.sigmoid(shifted)
        total = total + sharpness * sig * (1.0 - sig)
    return total


def contract_rows(left, right):
    return lax.dot_general(
        left, right, (((0,), (0,)), ((), ())), preferred_element_type=jnp.float32
    )


def contract_cols(left, right):
    return lax.dot_general(
        left, right, (((1,), (1,)), ((), ())), preferred_element_type=jnp.float32
    )


def on_device(tokens, grad_out, gate_prob, expert_ids, w_in, w_out, threshold, spike_counts):
    n_expert = lax.axis_size("expert")
    n_replica = lax.axis_size("dp")
    rows_local = spike_counts.shape[1]
    capacity = rows_local // n_expert
    width = tokens.shape[1]
    piece_width = width // n_replica
    select = selection(expert_ids[:, 0], n_expert, capacity)
    scaled = (gate_prob[:, None] * grad_out.astype(jnp.float32)).astype(jnp.bfloat16)
    send_x = (
        jnp.dot(select, tokens, preferred_element_type=jnp.float32)
        .astype(jnp.bfloat16)
        .reshape(n_expert, capacity, width)
    )
    send_g = (
        jnp.dot(select, scaled, preferred_element_type=jnp.float32)
        .astype(jnp.bfloat16)
        .reshape(n_expert, capacity, width)
    )
    local_in = w_in[0]
    local_out = w_out[0]
    limit = threshold[0]
    activity = (limit[None, :] * spike_counts[0].astype(jnp.float32) / STEPS).astype(jnp.bfloat16)
    full_in, full_out = (
        lax.all_gather(local_in, "dp", axis=0, tiled=True),
        lax.all_gather(local_out, "dp", axis=0, tiled=True),
    )
    recv_x, recv_g = (
        lax.all_to_all(send_x, "expert", split_axis=0, concat_axis=0, tiled=True),
        lax.all_to_all(send_g, "expert", split_axis=0, concat_axis=0, tiled=True),
    )
    rows_x = recv_x.reshape(rows_local, width)
    rows_g = recv_g.reshape(rows_local, width)
    membrane = jnp.dot(rows_x, full_in, preferred_element_type=jnp.float32)
    upstream = jnp.dot(rows_g, full_out, preferred_element_type=jnp.float32)
    grad_hidden = (upstream * surrogate(membrane, limit)).astype(jnp.bfloat16)
    back_rows = (
        contract_cols(grad_hidden, full_in).astype(jnp.bfloat16).reshape(n_expert, capacity, width)
    )
    cols_x, cols_g = (
        lax.all_to_all(
            recv_x.reshape(1, n_expert, capacity, width),
            "dp",
            split_axis=3,
            concat_axis=0,
            tiled=True,
        ),
        lax.all_to_all(
            recv_g.reshape(1, n_expert, capacity, width),
            "dp",
            split_axis=3,
            concat_axis=0,
            tiled=True,
        ),
    )
    all_hidden, all_activity = (
        lax.all_gather(grad_hidden, "dp", axis=0, tiled=True),
        lax.all_gather(activity, "dp", axis=0, tiled=True),
    )
    flat_x = cols_x.reshape(n_replica * rows_local, piece_width)
    flat_g = cols_g.reshape(n_replica * rows_local, piece_width)
    w_in_grad = contract_rows(flat_x, all_hidden).astype(jnp.bfloat16)[None]
    w_out_grad = contract_rows(flat_g, all_activity).astype(jnp.bfloat16)[None]
    returned = lax.all_to_all(back_rows, "expert", split_axis=0, concat_axis=0, tiled=True)
    returned = returned.reshape(n_expert * capacity, width)
    token_grad = contract_rows(select, returned).astype(jnp.bfloat16)
    return (token_grad, w_in_grad, w_out_grad)


def solution(mesh):
    placed = (
        P(("dp", "expert"), None),
        P(("dp", "expert"), None),
        P(("dp", "expert")),
        P(("dp", "expert"), None),
        P("expert", "dp", None),
        P("expert", "dp", None),
        P("expert", None),
        P("expert", "dp", None),
    )
    return jax.shard_map(
        on_device,
        mesh=mesh,
        in_specs=placed,
        out_specs=(P(("dp", "expert"), None), P("expert", "dp", None), P("expert", "dp", None)),
        check_vma=False,
    )
```

profile of v0, /device:TPU:1, one launch (start us, length us, event | category | flops | bytes accessed | tf_op | source)
XLA Modules:
  0.0 312.8 jit_solution(14199488935298154012)
XLA Ops:
  12.0 13.3 %all-to-all-start.1 = ((bf16[64,3,4096]{2,1,0:T(4,128)(2,1)}), bf16[64,3,4096]{2,1,0:T(4,128)(2,1)S(1)}, u32[]{:S(2)}, u32[]{:S(2)}) async-start(bf16[64,3,4096]{2,1,0:T(4,128)(2,1)} %reshape.50), calls=%async_computation.1 | async-start | bytes 4194304 | tf_op jit(solution)/shard_map/all_to_all | solution.py:72
  27.2 4.2 %reshape.48 = bf16[64,3,4096]{2,1,0:T(4,128)(2,1)} reshape(bf16[192,4096]{1,0:T(8,128)(2,1)} %convolution_convert_fusion.1) | data formatting | bytes 3145728 | tf_op jit(solution)/shard_map/reshape | solution.py:61
  31.4 43.6 %all-to-all-done.1 = bf16[64,3,4096]{2,1,0:T(4,128)(2,1)S(1)} async-done(((bf16[64,3,4096]{2,1,0:T(4,128)(2,1)}), bf16[64,3,4096]{2,1,0:T(4,128)(2,1)S(1)}, u32[]{:S(2)}, u32[]{:S(2)}) %all-to-all-start.1) | async-done | bytes 1572896 | tf_op jit(solution)/shard_map/all_to_all | solution.py:72
  75.0 7.2 %all-to-all-start = ((bf16[64,3,4096]{2,1,0:T(4,128)(2,1)}), bf16[64,3,4096]{2,1,0:T(4,128)(2,1)}, u32[]{:S(2)}, u32[]{:S(2)}) async-start(bf16[64,3,4096]{2,1,0:T(4,128)(2,1)} %reshape.48), calls=%async_computation | async-start | bytes 4194304 | tf_op jit(solution)/shard_map/all_to_all | solution.py:73
  82.2 5.0 %copy.21 = bf16[1,64,3,4096]{1,2,0,3:T(4,128)(2,1)} copy(bf16[1,64,3,4096]{3,2,1,0:T(4,128)(2,1)S(1)} %bitcast.54) | data formatting | bytes 3145728 | tf_op jit(solution)/shard_map/reshape | solution.py:85
  87.3 5.5 %reshape.60 = bf16[4,2,98304]{2,1,0:T(2,128)(2,1)} reshape(bf16[4096,1,3,64]{3,2,1,0:T(4,128)(2,1)} %bitcast.57) | data formatting | bytes 3145728
  92.8 39.1 %all-to-all-done = bf16[64,3,4096]{2,1,0:T(4,128)(2,1)} async-done(((bf16[64,3,4096]{2,1,0:T(4,128)(2,1)}), bf16[64,3,4096]{2,1,0:T(4,128)(2,1)}, u32[]{:S(2)}, u32[]{:S(2)}) %all-to-all-start) | async-done | bytes 1572896 | tf_op jit(solution)/shard_map/all_to_all | solution.py:73
  131.8 4.4 %all-to-all-start.3 = ((bf16[4,2,98304]{2,1,0:T(2,128)(2,1)}), bf16[4,2,98304]{2,1,0:T(2,128)(2,1)}, u32[]{:S(2)}, u32[]{:S(2)}) async-start(bf16[4,2,98304]{2,1,0:T(2,128)(2,1)} %reshape.60), calls=%async_computation.3 | async-start | bytes 3145728 | tf_op jit(solution)/shard_map/all_to_all | solution.py:84
  137.2 7.5 %copy.24 = bf16[1,64,3,4096]{1,2,0,3:T(4,128)(2,1)} copy(bf16[1,64,3,4096]{3,2,1,0:T(4,128)(2,1)} %bitcast.11) | data formatting | bytes 3145728 | tf_op jit(solution)/shard_map/reshape | solution.py:92
  144.7 5.5 %reshape.62 = bf16[4,2,98304]{2,1,0:T(2,128)(2,1)} reshape(bf16[4096,1,3,64]{3,2,1,0:T(4,128)(2,1)} %bitcast.58) | data formatting | bytes 3145728
  152.7 4.4 %reshape.49 = bf16[192,4096]{1,0:T(8,128)(2,1)} reshape(bf16[64,3,4096]{2,1,0:T(4,128)(2,1)} %all-to-all-done) | data formatting | bytes 3145728 | tf_op jit(solution)/shard_map/reshape | solution.py:76
  157.1 6.2 %fusion.2 = f32[192,1024]{1,0:T(8,128)} fusion(bf16[192,4096]{1,0:T(8,128)(2,1)S(1)} %copy-done.4, bf16[1,4096,1024]{2,1,0:T(8,128)(2,1)} %all-gather.13.cloned.1.call-done), kind=kOutput, calls=%fused_computation.2 | convolution fusion | flops 1610612736 | bytes 10747904 | tf_op jit(solution)/shard_map/dot_general | solution.py:77
  163.3 10.2 %all-to-all-done.3 = bf16[4,2,98304]{2,1,0:T(2,128)(2,1)} async-done(((bf16[4,2,98304]{2,1,0:T(2,128)(2,1)}), bf16[4,2,98304]{2,1,0:T(2,128)(2,1)}, u32[]{:S(2)}, u32[]{:S(2)}) %all-to-all-start.3) | async-done | bytes 1572896 | tf_op jit(solution)/shard_map/all_to_all | solution.py:84
  177.2 44.3 %all-gather.11.cloned.1.call-done = bf16[1,4096,1024]{2,1,0:T(8,128)(2,1)} async-done(((bf16[1,1024,1024]{2,1,0:T(8,128)(2,1)}), bf16[1,4096,1024]{2,1,0:T(8,128)(2,1)}) %all-gather.11.cloned.1.call-update) | async-done | bytes 8388624 | tf_op jit(solution)/shard_map/all_gather | solution.py:69
  221.5 6.6 %fusion.12 = bf16[192,1024]{1,0:T(8,128)(2,1)S(1)} fusion(bf16[192,4096]{1,0:T(8,128)(2,1)} %reshape.49, bf16[1,4096,1024]{2,1,0:T(8,128)(2,1)} %all-gather.11.cloned.1.call-done, f32[192,1024]{1,0:T(8,128)} %fusion.2, f32[1024]{0:T(1024)S(1)} %bitcast.65, f32[1024]{0:T(1024)S(1)} %bitcast.63, f32[1024]{0:T(1024)S(1)} %bitcast.64, f32[1024]{0:T(1024)S(1)} %bitcast.62), kind=kOutput, calls=%fused_computation.14 | convolution fusion | flops 1617887232 | bytes 11157504 | tf_op jit(solution)/shard_map/dot_general | solution.py:78
  228.2 7.6 %fusion.6 = bf16[192,4096]{1,0:T(8,128)(2,1)} fusion(bf16[192,1024]{1,0:T(8,128)(2,1)S(1)} %fusion.12, bf16[1,4096,1024]{2,1,0:T(8,128)(2,1)} %all-gather.13.cloned.1.call-done), kind=kOutput, calls=%fused_computation.6 | convolution fusion | flops 1611399168 | bytes 10354688 | tf_op jit(solution)/shard_map/dot_general | solution.py:39
  235.8 4.1 %reshape.52 = bf16[64,3,4096]{2,1,0:T(4,128)(2,1)} reshape(bf16[192,4096]{1,0:T(8,128)(2,1)} %fusion.6) | data formatting | bytes 3145728 | tf_op jit(solution)/shard_map/reshape | solution.py:81
  241.0 10.9 %all-to-all-start.2 = ((bf16[64,3,4096]{2,1,0:T(4,128)(2,1)}), bf16[64,3,4096]{2,1,0:T(4,128)(2,1)}, u32[]{:S(2)}, u32[]{:S(2)}) async-start(bf16[64,3,4096]{2,1,0:T(4,128)(2,1)} %reshape.52), calls=%async_computation.2 | async-start | bytes 4194304 | tf_op jit(solution)/shard_map/all_to_all | solution.py:107
  252.5 5.4 %reshape.61 = bf16[4096,1,3,64]{3,2,1,0:T(4,128)(2,1)} reshape(bf16[4,2,98304]{2,1,0:T(2,128)(2,1)} %all-to-all-done.3) | data formatting | bytes 3145728
  257.9 7.1 %copy.27 = bf16[1,64,3,4,1024]{4,3,1,2,0:T(4,128)(2,1)} copy(bf16[1,64,3,4,1024]{1,2,4,3,0:T(4,128)(2,1)} %bitcast.55) | data formatting | bytes 3145728 | tf_op jit(solution)/shard_map/all_to_all | solution.py:84
  270.2 5.4 %reshape.63 = bf16[4096,1,3,64]{3,2,1,0:T(4,128)(2,1)} reshape(bf16[4,2,98304]{2,1,0:T(2,128)(2,1)} %copy-done.2) | data formatting | bytes 3145728
  275.6 7.1 %copy.28 = bf16[1,64,3,4,1024]{4,3,1,2,0:T(4,128)(2,1)} copy(bf16[1,64,3,4,1024]{1,2,4,3,0:T(4,128)(2,1)} %bitcast.56) | data formatting | bytes 3145728 | tf_op jit(solution)/shard_map/all_to_all | solution.py:91
  288.0 5.2 %convert_bitcast_fusion = bf16[1,1024,1024]{2,1,0:T(8,128)(2,1)} fusion(bf16[768,1024]{1,0:T(8,128)(2,1)} %reshape.57, bf16[768,1024]{1,0:T(8,128)(2,1)} %all-gather.9.cloned.1.call-done), kind=kOutput, calls=%fused_computation.10 | convolution fusion | flops 1611661312 | bytes 5242880 | tf_op jit(solution)/shard_map/dot_general | solution.py:33
  293.2 4.6 %convert_bitcast_fusion.1 = bf16[1,1024,1024]{2,1,0:T(8,128)(2,1)} fusion(bf16[768,1024]{1,0:T(8,128)(2,1)S(1)} %copy-done.3, bf16[768,1024]{1,0:T(8,128)(2,1)} %all-gather.7.cloned.1.call-done), kind=kOutput, calls=%fused_computation.11 | convolution fusion | flops 1611661312 | bytes 5242880 | tf_op jit(solution)/shard_map/dot_general | solution.py:33
  (52 shorter events, 34.6 us)
Async XLA Ops:
  7.2 2.0 copy-start
  7.2 149.9 %all-gather.13.cloned.1.call-start = ((), (), s32[]{:S(2)}) async-start(), calls=%async_computation.8 | async-start | bytes 10485760 | tf_op jit(solution)/shard_map/all_gather | solution.py:68
  7.9 0.8 copy-start.9
  7.9 213.6 %all-gather.11.cloned.1.call-start = ((), (), s32[]{:S(2)}) async-start(), calls=%async_computation.7 | async-start | bytes 10485760 | tf_op jit(solution)/shard_map/all_gather | solution.py:69
  12.0 13.3 %copy-start.5 = (bf16[128,4096]{1,0:T(8,128)(2,1)S(1)}, bf16[128,4096]{1,0:T(8,128)(2,1)}, u32[]{:S(2)}) copy-start(bf16[128,4096]{1,0:T(8,128)(2,1)} %param.9) | copy-start | bytes 3145732
  12.0 13.3 %copy-start.10 = (f32[128]{0:T(128)S(1)}, f32[128]{0:T(128)}, u32[]{:S(2)}) copy-start(f32[128]{0:T(128)} %param.10) | copy-start | bytes 1540
  12.0 63.0 %all-to-all-start.1 = ((bf16[64,3,4096]{2,1,0:T(4,128)(2,1)}), bf16[64,3,4096]{2,1,0:T(4,128)(2,1)S(1)}, u32[]{:S(2)}, u32[]{:S(2)}) async-start(bf16[64,3,4096]{2,1,0:T(4,128)(2,1)} %reshape.50), calls=%async_computation.1 | async-start | bytes 4194304 | tf_op jit(solution)/shard_map/all_to_all | solution.py:72
  75.0 56.8 %all-to-all-start = ((bf16[64,3,4096]{2,1,0:T(4,128)(2,1)}), bf16[64,3,4096]{2,1,0:T(4,128)(2,1)}, u32[]{:S(2)}, u32[]{:S(2)}) async-start(bf16[64,3,4096]{2,1,0:T(4,128)(2,1)} %reshape.48), calls=%async_computation | async-start | bytes 4194304 | tf_op jit(solution)/shard_map/all_to_all | solution.py:73
  92.7 43.5 %copy-start.6 = (s32[1,192,1024]{2,1,0:T(8,128)S(1)}, s32[1,192,1024]{2,1,0:T(8,128)}, u32[]{:S(2)}) copy-start(s32[1,192,1024]{2,1,0:T(8,128)} %param.15) | copy-start | bytes 2359300
  92.8 43.5 %copy-start.8 = (f32[1,1024]{1,0:T(1,128)S(1)}, f32[1,1024]{1,0:T(1,128)}, u32[]{:S(2)}) copy-start(f32[1,1024]{1,0:T(1,128)} %param.14) | copy-start | bytes 12292
  131.8 41.7 %all-to-all-start.3 = ((bf16[4,2,98304]{2,1,0:T(2,128)(2,1)}), bf16[4,2,98304]{2,1,0:T(2,128)(2,1)}, u32[]{:S(2)}, u32[]{:S(2)}) async-start(bf16[4,2,98304]{2,1,0:T(2,128)(2,1)} %reshape.60), calls=%async_computation.3 | async-start | bytes 3145728 | tf_op jit(solution)/shard_map/all_to_all | solution.py:84
  136.2 151.8 %all-gather.9.cloned.1.call-start = ((), (), s32[]{:S(2)}) async-start(), calls=%async_computation.6 | async-start | bytes 1966080 | tf_op jit(solution)/shard_map/all_gather | solution.py:101
  152.7 4.4 %copy-start.4 = (bf16[192,4096]{1,0:T(8,128)(2,1)S(1)}, bf16[192,4096]{1,0:T(8,128)(2,1)}, u32[]{:S(2)}) copy-start(bf16[192,4096]{1,0:T(8,128)(2,1)} %reshape.51) | copy-start | bytes 4718596
  173.5 66.4 %all-to-all-start.4 = ((bf16[4,2,98304]{2,1,0:T(2,128)(2,1)}), bf16[4,2,98304]{2,1,0:T(2,128)(2,1)S(1)}, u32[]{:S(2)}, u32[]{:S(2)}) async-start(bf16[4,2,98304]{2,1,0:T(2,128)(2,1)} %reshape.62), calls=%async_computation.4 | async-start | bytes 3145728 | tf_op jit(solution)/shard_map/all_to_all | solution.py:91
  228.2 7.6 %copy-start.7 = (bf16[192,1024]{1,0:T(8,128)(2,1)}, bf16[192,1024]{1,0:T(8,128)(2,1)S(1)}, u32[]{:S(2)}) copy-start(bf16[192,1024]{1,0:T(8,128)(2,1)S(1)} %fusion.12) | copy-start | bytes 1179652
  239.9 1.1 copy-start.2
  241.0 60.5 %all-to-all-start.2 = ((bf16[64,3,4096]{2,1,0:T(4,128)(2,1)}), bf16[64,3,4096]{2,1,0:T(4,128)(2,1)}, u32[]{:S(2)}, u32[]{:S(2)}) async-start(bf16[64,3,4096]{2,1,0:T(4,128)(2,1)} %reshape.52), calls=%async_computation.2 | async-start | bytes 4194304 | tf_op jit(solution)/shard_map/all_to_all | solution.py:107
  251.9 41.2 %all-gather.7.cloned.1.call-start = ((), (), s32[]{:S(2)}) async-start(), calls=%async_computation.5 | async-start | bytes 1966080 | tf_op jit(solution)/shard_map/all_gather | solution.py:100
  288.0 5.2 %copy-start.3 = (bf16[768,1024]{1,0:T(8,128)(2,1)S(1)}, bf16[768,1024]{1,0:T(8,128)(2,1)}, u32[]{:S(2)}) copy-start(bf16[768,1024]{1,0:T(8,128)(2,1)} %reshape.55) | copy-start | bytes 4718596
  301.5 4.7 %copy-start.1 = (bf16[128,4096]{1,0:T(8,128)(2,1)S(1)}, bf16[128,4096]{1,0:T(8,128)(2,1)}, u32[]{:S(2)}) copy-start(bf16[128,4096]{1,0:T(8,128)(2,1)} %param.8) | copy-start | bytes 3145732
Sparse Core Ops, SparseCore 0:
  9.8 89.4 all-gather.12
  101.1 120.3 all-gather.10
  223.3 30.0 all-gather.8
  255.7 29.1 all-gather.6
where the time goes:
time: 315 us; the launch traced here: 313 us
  waiting for transfers between devices  143 us (45%)
  local copies, waits for them, and re-layouts  80.9 us (26%)
  starting transfers between devices  39.9 us (13%)
  matrix products  34 us (11%)
  between operations  13.9 us (4%)
    all_gather x1, waiting for transfers between devices, on_device(): lax.all_gather(local_out, 'dp', axis=0, tiled=True)  44.3 us
    all_to_all x1, waiting for transfers between devices, on_device(): lax.all_to_all(send_x, 'expert', split_axis=0, concat_axis=0, tiled=True)  43.6 us
    all_to_all x1, waiting for transfers between devices, on_device(): lax.all_to_all(send_g, 'expert', split_axis=0, concat_axis=0, tiled=True)  39.1 us
    unnamed x26, local copies, waits for them, and re-layouts  23 us
    all_to_all x1, starting transfers between devices, on_device(): lax.all_to_all(send_x, 'expert', split_axis=0, concat_axis=0, tiled=True)  13.3 us
    dot_general x3, matrix products, contract_rows(): lax.dot_general(left, right, (((0,), (0,)), ((), ())), preferred_element_...  11.2 us
    all_to_all x1, starting transfers between devices, on_device(): lax.all_to_all(back_rows, 'expert', split_axis=0, concat_axis=0, tiled=True)  10.9 us
    all_to_all x1, waiting for transfers between devices, on_device(): lax.all_to_all(recv_x.reshape(1, n_expert, capacity, width), 'dp', split_...  10.2 us
  transfers between devices with their start and end apart: 9, of which 5 were waited for; matrix products, arithmetic and copies ran while one was open for 35% of the time, Pallas kernels for 0%

commit v1 on v0

v1 whole, which is shorter than its diff:
```python
import functools
import jax
import jax.numpy as jnp
from jax import lax
from jax.experimental import pallas as pl
from jax.experimental.pallas import tpu as pltpu
from jax.sharding import PartitionSpec as P

STEPS = 4
SHARP = 4.0
TOK = 128
CAP = 3
NE = 64
ND = 4
W = 1024
FF = 1024
HALF = 512
MAIN = 384
PIECE = 128
NC = 4
KC = 16
ROWS = 192
HOME = 48
MROWS = KC * 16
F32, BF16, I32 = jnp.float32, jnp.bfloat16, jnp.int32
MESH = pl.DeviceIdType.MESH


def dot(a, b, dims=((1,), (0,))):
    return lax.dot_general(a, b, (dims, ((), ())), preferred_element_type=F32)


def one_hot(cond):
    return jnp.where(cond, 1.0, 0.0).astype(BF16)


def row_parts(p):
    rr = (p >= 48).astype(I32) + (p >= 96).astype(I32) + (p >= 144).astype(I32)
    pp = p - 48 * rr
    kk = (pp * 171) >> 9
    return rr, kk, pp - 3 * kk


def spread(p, q, m):
    rr, kk, c3 = row_parts(p)
    rho = rr * 3 + c3
    if m is None:
        return q == kk * 16 + rho
    return (q == kk * 16 + 12 + (rho & 3)) & ((rho >> 2) == m)


def kernel(
    gate, ids, limit, tokens, grads, w_in, w_out, spikes,
    tok_out, win_out, wout_out,
    grad_v, scaled, spike_v, win_v, wout_v, pos_v, xin, sel0, sel1, p0, p1, pt0, pt1,
    fsend, frecv, rows, msend, mrecv, uown, usend, urecv, hid, act, rsend, rrecv, tsend, wg,
    lsem, pos_s, pos_r, x_s, x_r, f_s, f_r, m_s, m_r, u_s, u_r, h_s, h_r, a_s, a_r, r_s, r_r, t_s, t_r, w_s,
):
    r = lax.axis_index("dp")
    e = lax.axis_index("expert")
    z, y, c = e // 8, (e // 2) % 4, e % 2

    def there(k):
        dy, dz, dc = k // 16, (k // 2) % 8, k % 2
        return (r, ((z + dz) % 8) * 8 + ((y + dy) % 4) * 2 + (c + dc) % 2)

    def back(k):
        dy, dz, dc = k // 16, (k // 2) % 8, k % 2
        return (r, ((z + 8 - dz) % 8) * 8 + ((y + 4 - dy) % 4) * 2 + (c + dc) % 2)

    def replica(d):
        return (r + d) % ND

    def remote(src, dst, ss, rs, device):
        return pltpu.make_async_remote_copy(
            src_ref=src, dst_ref=dst, send_sem=ss, recv_sem=rs, device_id=device, device_id_type=MESH
        )

    def arrived(ref, ss, rs):
        remote(ref, ref, ss, rs, (replica(1), e)).wait_recv()

    def sent(ref, ss, rs):
        remote(ref, ref, ss, rs, (replica(1), e)).wait_send()

    def order(i):
        dzi = i // 2
        half = dzi // 2
        return (half + (dzi % 2) * (7 - 2 * half)) * 2 + i % 2

    load_g = pltpu.make_async_copy(grads, grad_v, lsem.at[0])
    load_g.start()
    load_in = pltpu.make_async_copy(w_in, win_v, lsem.at[1])
    load_in.start()
    load_out = pltpu.make_async_copy(w_out, wout_v, lsem.at[2])
    load_out.start()
    load_s = pltpu.make_async_copy(spikes, spike_v, lsem.at[3])
    load_s.start()

    barrier = pltpu.get_barrier_semaphore()

    @pl.loop(1, NE)
    def _(k):
        pl.semaphore_signal(barrier, inc=1, device_id=there(k), device_id_type=MESH)

    for d in range(1, ND):
        pl.semaphore_signal(barrier, inc=1, device_id=(replica(d), e), device_id_type=MESH)

    col = ids[...]
    ti = lax.broadcasted_iota(I32, (TOK, TOK), 0)
    tj = lax.broadcasted_iota(I32, (TOK, TOK), 1)
    row = jnp.sum(jnp.where(ti == tj, col, 0), axis=0, keepdims=True)
    slot = jnp.sum(jnp.where((col == row) & (ti < tj), 1, 0), axis=0, keepdims=True)
    kidx = ((((row >> 1) & 3) - y) & 3) * 16 + (((row >> 3) - z) & 7) * 2 + ((row & 1) ^ c)
    pos = kidx * 16 + r * CAP + slot
    pos_v[r] = jnp.broadcast_to(pos, (8, TOK))

    pl.semaphore_wait(barrier, NE - 1 + ND - 1)

    for d in (2, 1, 3):
        remote(pos_v.at[r], pos_v.at[r], pos_s, pos_r, (replica(d), e)).start()

    def exchange(a, h, source):
        mine = xin.at[a, pl.ds(pl.multiple_of(r * TOK, TOK), TOK), pl.ds(h * HALF, HALF)]

        def piece(q):
            return source.at[:, pl.ds(pl.multiple_of(q * W + h * HALF, HALF), HALF)]

        pltpu.make_async_copy(piece(r), mine, x_r.at[a, h]).start()
        for d in (2, 1, 3):
            remote(piece(replica(d)), mine, x_s.at[a, h], x_r.at[a, h], (replica(d), e)).start()

    exchange(0, 0, tokens)
    exchange(0, 1, tokens)

    load_g.wait()
    gate_col = jnp.sum(jnp.where(ti == tj, gate[...], 0.0), axis=1, keepdims=True)

    @pl.loop(0, 8)
    def _(i):
        cols = pl.ds(pl.multiple_of(i * 512, 512), 512)
        scaled[:, cols] = (gate_col * grad_v[:, cols].astype(F32)).astype(BF16)

    pi = lax.broadcasted_iota(I32, (ROWS, MROWS), 0)
    qi = lax.broadcasted_iota(I32, (ROWS, MROWS), 1)
    p0[...] = one_hot(spread(pi, qi, None))
    for m in range(3):
        p1[m] = one_hot(spread(pi, qi, m))
    pi = lax.broadcasted_iota(I32, (MROWS, ROWS), 1)
    qi = lax.broadcasted_iota(I32, (MROWS, ROWS), 0)
    pt0[...] = one_hot(spread(pi, qi, None))
    for m in range(3):
        pt1[m] = one_hot(spread(pi, qi, m))

    arrived(pos_v.at[pl.ds(0, 3)], pos_s, pos_r)

    @pl.loop(0, NC)
    def _(ch):
        base = ch * MROWS
        qi = lax.broadcasted_iota(I32, (MROWS, TOK), 0) + base
        at = pl.ds(pl.multiple_of(base, MROWS), MROWS)
        for q in range(ND):
            where = pos_v[q][0:1]
            rho = where & 15
            tail = where - rho + 12 + (rho & 3)
            cols = slice(q * TOK, (q + 1) * TOK)
            sel0[at, cols] = one_hot(qi == where)
            for m in range(3):
                sel1[m, at, cols] = one_hot(qi == jnp.where((rho >> 2) == m, tail, -1))

    def select(a, h, ch):
        at = pl.ds(pl.multiple_of(ch * MROWS, MROWS), MROWS)
        main = dot(sel0[at, :], xin[a, :, h * HALF : h * HALF + MAIN])
        tail = xin[a, :, h * HALF + MAIN : (h + 1) * HALF]
        for m in range(3):
            cols = slice(m * PIECE, (m + 1) * PIECE)
            both = main[:, cols] + dot(sel1[m, at, :], tail)
            fsend[a, pl.ds(ch * KC, KC), h, :, cols] = both.astype(BF16).reshape(KC, 16, PIECE)

    def deliver(ch, src, dst, ss, rs, target):
        @pl.loop(0, KC)
        def _(i):
            k = ch * KC + order(i)

            @pl.when(k == 0)
            def _():
                pltpu.make_async_copy(src(k), dst(k), rs).start()

            @pl.when(k != 0)
            def _():
                remote(src(k), dst(k), ss, rs, target(k)).start()

    for h in range(2):
        arrived(xin.at[0, :, pl.ds(h * HALF, HALF)], x_s.at[0, h], x_r.at[0, h])

        @pl.loop(0, NC)
        def _(ch):
            select(0, h, ch)
            deliver(
                ch, lambda k: fsend.at[0, k, h], lambda k: frecv.at[0, k, h], f_s.at[0], f_r.at[h * NC + ch], there
            )

        if h == 0:
            exchange(1, 0, scaled)
            exchange(1, 1, scaled)

    load_s.wait()
    pi = lax.broadcasted_iota(I32, (ROWS, ROWS), 0)
    qi = lax.broadcasted_iota(I32, (ROWS, ROWS), 1)
    dy, kk, c3 = row_parts(pi)
    origin = (((z - (kk >> 1)) & 7) * 8 + ((y - dy) & 3) * 2 + (c ^ (kk & 1))) * CAP + c3
    natural = (limit[...] * spike_v[...].astype(F32) / STEPS).astype(BF16)
    ordered = dot(one_hot(qi == origin), natural).astype(BF16)
    for ch in range(NC):
        act[ch, r] = ordered[ch * HOME : (ch + 1) * HOME]

    for h in range(2):
        arrived(xin.at[1, :, pl.ds(h * HALF, HALF)], x_s.at[1, h], x_r.at[1, h])

    @pl.loop(0, NC)
    def _(ch):
        select(1, 0, ch)
        select(1, 1, ch)
        deliver(ch, lambda k: fsend.at[1, k], lambda k: frecv.at[1, k], f_s.at[1], f_r.at[2 * NC + ch], there)

    for d in (2, 1, 3):
        remote(act.at[:, r], act.at[:, r], a_s, a_r, (replica(d), e)).start()

    load_in.wait()
    load_out.wait()

    def compact(a, ch):
        at = pl.ds(pl.multiple_of(ch * ROWS, ROWS), ROWS)
        for h in range(2):
            block = frecv[a, pl.ds(ch * KC, KC), h].reshape(MROWS, MAIN)
            rows[a, at, h * HALF : h * HALF + MAIN] = dot(p0[...], block).astype(BF16)
            tail = sum(dot(p1[m], block[:, m * PIECE : (m + 1) * PIECE]) for m in range(3))
            rows[a, at, h * HALF + MAIN : (h + 1) * HALF] = tail.astype(BF16)
        return rows[a, at, :]

    @pl.loop(0, NC)
    def _(ch):
        arrived(frecv.at[0, pl.ds(ch * KC, KC), 0], f_s.at[0], f_r.at[ch])
        arrived(frecv.at[0, pl.ds(ch * KC, KC), 1], f_s.at[0], f_r.at[NC + ch])
        msend[ch] = dot(compact(0, ch), win_v[...]).reshape(ND, HOME, FF)
        for d in (2, 1, 3):
            q = replica(d)
            remote(msend.at[ch, q], mrecv.at[ch, d - 1], m_s, m_r.at[ch], (q, e)).start()

    def upstream(ch):
        arrived(frecv.at[1, pl.ds(ch * KC, KC)], f_s.at[1], f_r.at[2 * NC + ch])
        part = dot(compact(1, ch), wout_v[...]).reshape(ND, HOME, FF)
        uown[...] = part
        usend[ch] = part.astype(BF16)
        for d in (2, 1, 3):
            q = replica(d)
            remote(usend.at[ch, q], urecv.at[ch, d - 1], u_s, u_r.at[ch], (q, e)).start()

    def hidden(ch):
        arrived(mrecv.at[ch], m_s, m_r.at[ch])
        arrived(urecv.at[ch], u_s, u_r.at[ch])

        @pl.loop(0, 3)
        def _(i):
            at = pl.ds(pl.multiple_of(i * 16, 16), 16)
            membrane = msend[ch, r, at] + mrecv[ch, 0, at] + mrecv[ch, 1, at] + mrecv[ch, 2, at]
            up = uown[r, at]
            for d in range(3):
                up = up + urecv[ch, d, at].astype(F32)
            total = jnp.zeros_like(membrane)
            for step in range(STEPS):
                sig = jax.nn.sigmoid(SHARP * (membrane - (step + 0.5) * limit[...]))
                total = total + SHARP * sig * (1.0 - sig)
            hid[ch, r, at] = (up * total).astype(BF16)

        for d in (2, 1, 3):
            remote(hid.at[ch, r], hid.at[ch, r], h_s, h_r.at[ch], (replica(d), e)).start()

    def slot_grad(ch):
        arrived(hid.at[ch, pl.ds(0, 3)], h_s, h_r.at[ch])
        sg = dot(hid[ch].reshape(ROWS, FF), win_v[...], ((1,), (1,))).astype(BF16)
        for h in range(2):
            main = dot(pt0[...], sg[:, h * HALF : h * HALF + MAIN])
            tail = sg[:, h * HALF + MAIN : (h + 1) * HALF]
            for m in range(3):
                cols = slice(m * PIECE, (m + 1) * PIECE)
                both = main[:, cols] + dot(pt1[m], tail)
                rsend[h, pl.ds(ch * KC, KC), :, cols] = both.astype(BF16).reshape(KC, 16, PIECE)

    def give_back(h, ch):
        deliver(ch, lambda k: rsend.at[h, k], lambda k: rrecv.at[h, k], r_s.at[h], r_r.at[h], back)

    @pl.loop(0, NC)
    def _(ch):
        upstream(ch)

        @pl.when(ch > 0)
        def _():
            slot_grad(ch - 1)
            give_back(0, ch - 1)

        hidden(ch)

    def weight_grad(a, right, out):
        @pl.loop(0, 4)
        def _(i):
            at = pl.ds(pl.multiple_of(i * 256, 256), 256)
            wg[a, at, :] = dot(rows[a, :, at], right[...].reshape(NC * ROWS, FF), ((0,), (0,))).astype(BF16)

        pltpu.make_async_copy(wg.at[a], out, w_s.at[a]).start()

    slot_grad(NC - 1)
    give_back(0, NC - 1)

    @pl.loop(0, NC)
    def _(ch):
        give_back(1, ch)

    weight_grad(0, hid, win_out)
    arrived(act.at[:, pl.ds(0, 3)], a_s, a_r)
    weight_grad(1, act, wout_out)

    for h in range(2):
        arrived(rrecv.at[h], r_s.at[h], r_r.at[h])
        block = rrecv[h].reshape(NC * MROWS, MAIN)
        tsend[h, :, 0:MAIN] = dot(sel0[...], block, ((0,), (0,))).astype(BF16)
        tail = sum(dot(sel1[m], block[:, m * PIECE : (m + 1) * PIECE], ((0,), (0,))) for m in range(3))
        tsend[h, :, MAIN:HALF] = tail.astype(BF16)
        place = tok_out.at[:, pl.ds(pl.multiple_of(r * W + h * HALF, HALF), HALF)]

        def part(q):
            return tsend.at[h, pl.ds(pl.multiple_of(q * TOK, TOK), TOK)]

        pltpu.make_async_copy(part(r), place, t_r.at[h]).start()
        for d in (2, 1, 3):
            q = replica(d)
            remote(part(q), place, t_s.at[h], t_r.at[h], (q, e)).start()

    sent(pos_v.at[pl.ds(0, 3)], pos_s, pos_r)
    for a in range(2):
        for h in range(2):
            sent(xin.at[a, pl.ds(0, 3 * TOK), pl.ds(h * HALF, HALF)], x_s.at[a, h], x_r.at[a, h])
        sent(fsend.at[a, pl.ds(1, NE - 1)], f_s.at[a], f_r.at[0])
    sent(msend.at[pl.ds(0, 3)], m_s, m_r.at[0])
    sent(usend.at[pl.ds(0, 3)], u_s, u_r.at[0])
    sent(hid.at[pl.ds(0, 3)], h_s, h_r.at[0])
    sent(act.at[:, pl.ds(0, 3)], a_s, a_r)
    for h in range(2):
        sent(rsend.at[h, pl.ds(1, NE - 1)], r_s.at[h], r_r.at[h])
        sent(tsend.at[h, pl.ds(0, 3 * TOK)], t_s.at[h], t_r.at[h])
    for a, out in enumerate((win_out, wout_out)):
        pltpu.make_async_copy(wg.at[a], out, w_s.at[a]).wait()
    for h in range(2):
        arrived(tok_out.at[:, pl.ds(0, ND * HALF)], t_s.at[h], t_r.at[h])


def on_device(tokens, grad_out, gate_prob, expert_ids, w_in, w_out, threshold, spike_counts):
    vmem = pl.BlockSpec(memory_space=pltpu.VMEM)
    hbm = pl.BlockSpec(memory_space=pl.ANY)
    dma = pltpu.SemaphoreType.DMA
    out = pl.pallas_call(
        kernel,
        name="moe_backward",
        out_shape=(
            jax.ShapeDtypeStruct((TOK, ND * W), BF16),
            jax.ShapeDtypeStruct((W, FF), BF16),
            jax.ShapeDtypeStruct((W, FF), BF16),
        ),
        in_specs=[vmem, vmem, vmem] + [hbm] * 5,
        out_specs=(hbm, hbm, hbm),
        scratch_shapes=[
            pltpu.VMEM((TOK, ND * W), BF16),
            pltpu.VMEM((TOK, ND * W), BF16),
            pltpu.VMEM((ROWS, FF), I32),
            pltpu.VMEM((W, FF), BF16),
            pltpu.VMEM((W, FF), BF16),
            pltpu.VMEM((ND, 8, TOK), I32),
            pltpu.VMEM((2, ND * TOK, W), BF16),
            pltpu.VMEM((NC * MROWS, ND * TOK), BF16),
            pltpu.VMEM((3, NC * MROWS, ND * TOK), BF16),
            pltpu.VMEM((ROWS, MROWS), BF16),
            pltpu.VMEM((3, ROWS, MROWS), BF16),
            pltpu.VMEM((MROWS, ROWS), BF16),
            pltpu.VMEM((3, MROWS, ROWS), BF16),
            pltpu.VMEM((2, NE, 2, 16, MAIN), BF16),
            pltpu.VMEM((2, NE, 2, 16, MAIN), BF16),
            pltpu.VMEM((2, NC * ROWS, W), BF16),
            pltpu.VMEM((NC, ND, HOME, FF), F32),
            pltpu.VMEM((NC, 3, HOME, FF), F32),
            pltpu.VMEM((ND, HOME, FF), F32),
            pltpu.VMEM((NC, ND, HOME, FF), BF16),
            pltpu.VMEM((NC, 3, HOME, FF), BF16),
            pltpu.VMEM((NC, ND, HOME, FF), BF16),
            pltpu.VMEM((NC, ND, HOME, FF), BF16),
            pltpu.VMEM((2, NE, 16, MAIN), BF16),
            pltpu.VMEM((2, NE, 16, MAIN), BF16),
            pltpu.VMEM((2, ND * TOK, HALF), BF16),
            pltpu.VMEM((2, W, FF), BF16),
            dma((4,)),
            dma, dma,
            dma((2, 2)), dma((2, 2)),
            dma((2,)), dma((3 * NC,)),
            dma, dma((NC,)),
            dma, dma((NC,)),
            dma, dma((NC,)),
            dma, dma,
            dma((2,)), dma((2,)),
            dma((2,)), dma((2,)),
            dma((2,)),
        ],
        compiler_params=pltpu.CompilerParams(
            collective_id=0, has_side_effects=True, vmem_limit_bytes=58 << 20
        ),
        cost_estimate=pl.CostEstimate(flops=9 * 10**9, bytes_accessed=14 << 20, transcendentals=1 << 20),
    )(
        gate_prob.reshape(1, TOK), expert_ids, threshold, tokens, grad_out,
        w_in.reshape(W, FF), w_out.reshape(W, FF), spike_counts.reshape(ROWS, FF),
    )
    return out[0], out[1][None], out[2][None]


def solution(mesh):
    placed = (
        P(("dp", "expert"), None),
        P(("dp", "expert"), None),
        P(("dp", "expert")),
        P(("dp", "expert"), None),
        P("expert", "dp", None),
        P("expert", "dp", None),
        P("expert", None),
        P("expert", "dp", None),
    )
    return jax.shard_map(
        on_device,
        mesh=mesh,
        in_specs=placed,
        out_specs=(P(("dp", "expert"), None), P("expert", "dp", None), P("expert", "dp", None)),
        check_vma=False,
    )
```

time: 315 us -> 186 us (0.59)
  Pallas kernels: 0 us -> 177 us
  waiting for transfers between devices: 143 us -> 0 us
  local copies, waits for them, and re-layouts: 80.9 us -> 7.5 us
  starting transfers between devices: 39.9 us -> 0 us
  matrix products: 34 us -> 0 us
  between operations: 13.9 us -> 0.65 us
    pallas_call x0 -> x1, Pallas kernels: none -> 177 us  [on_device(): pl.pallas_call(kernel, name='moe_backward', out_shape=(jax.ShapeDtypeStru...]
    all_to_all x5 -> x0, waiting for transfers between devices: 96.7 us -> none  [the longest x1 43.6 us: on_device(): lax.all_to_all(send_x, 'expert', split_axis=0, concat_axis=0, tiled=True)]
    all_gather x4 -> x0, waiting for transfers between devices: 44.3 us -> none  [the longest x1 44.3 us: on_device(): lax.all_gather(local_out, 'dp', axis=0, tiled=True)]
    all_to_all x5 -> x0, starting transfers between devices: 39.5 us -> none  [the longest x1 13.3 us: on_device(): lax.all_to_all(send_x, 'expert', split_axis=0, concat_axis=0, tiled=True)]
    reshape x10 -> x0, local copies, waits for them, and re-layouts: 38.3 us -> none  [the longest x1 7.48 us: on_device(): recv_g.reshape(1, n_expert, capacity, width)]
    dot_general x8 -> x0, matrix products: 34 us -> none  [the longest x3 11.2 us: contract_rows(): lax.dot_general(left, right, (((0,), (0,)), ((), ())), preferred_element_...]
    all_to_all x4 -> x0, local copies, waits for them, and re-layouts: 19.7 us -> none  [the longest x2 9.86 us: on_device(): lax.all_to_all(recv_g.reshape(1, n_expert, capacity, width), 'dp', split_...]
    unnamed x26 -> x8, local copies, waits for them, and re-layouts: 23 us -> 7.5 us
  transfers between devices with their start and end apart: 9 -> 0, of which waited for: 5 -> 0; matrix products, arithmetic and copies ran while one was open for 35% -> 0% of each run, Pallas kernels for 0% -> 0%
where the time goes in v1:
time: 186 us; the launch traced here: 185 us
  Pallas kernels  177 us (95%)
  local copies, waits for them, and re-layouts  7.5 us (4%)
    pallas_call x1, Pallas kernels, on_device(): pl.pallas_call(kernel, name='moe_backward', out_shape=(jax.ShapeDtypeStru...  177 us
    unnamed x8, local copies, waits for them, and re-layouts  7.5 us

profile of v1, /device:TPU:1, one launch (start us, length us, event | category | flops | bytes accessed | tf_op | source)
XLA Modules:
  0.0 185.4 jit_solution(6938876573165006576)
XLA Ops:
  0.6 1.4 copy.11.ids
  2.0 177.3 %moe_backward.1 = (bf16[128,4096]{1,0:T(8,128)(2,1)}, bf16[1024,1024]{1,0:T(8,128)(2,1)}, bf16[1024,1024]{1,0:T(8,128)(2,1)}) custom-call(f32[1,128]{1,0:T(1,128)} %bitcast.11, s32[128,1]{1,0:T(8,128)} %copy.11.ids, f32[1,1024]{1,0:T(1,128)} %limit.1, bf16[128,4096]{1,0:T(8,128)(2,1)} %tokens.1, bf16[128,4096]{1,0:T(8,128)(2,1)} %grads.1, ...), custom_call_target="tpu_custom_call" | custom-call | flops 8999999488 | bytes 14680064 | tf_op jit(solution)/shard_map/moe_backward/pallas_call | solution.py:360
  179.3 0.0 copy-start.1
  179.3 2.4 %copy.15 = bf16[128,4096]{1,0:T(8,128)(2,1)} copy(bf16[128,4096]{1,0:T(8,128)(2,1)} %get-tuple-element.12) | data formatting | bytes 2097152
  181.8 0.0 copy-done.1
  181.8 0.0 copy-start
  181.8 1.3 copy.16
  183.1 1.0 copy-done
  184.1 1.3 copy.17
Async XLA Ops:
  179.3 2.4 %copy-start.1 = (bf16[1024,1024]{1,0:T(8,128)(2,1)S(1)}, bf16[1024,1024]{1,0:T(8,128)(2,1)}, u32[]{:S(2)}) copy-start(bf16[1024,1024]{1,0:T(8,128)(2,1)} %get-tuple-element.7) | copy-start | bytes 6291460
  181.8 2.3 %copy-start = (bf16[1024,1024]{1,0:T(8,128)(2,1)S(1)}, bf16[1024,1024]{1,0:T(8,128)(2,1)}, u32[]{:S(2)}) copy-start(bf16[1024,1024]{1,0:T(8,128)(2,1)} %get-tuple-element.8) | copy-start | bytes 6291460

commit v2 on v1

--- a/solution.py
+++ b/solution.py
@@ -105,10 +105,10 @@
     for d in range(1, ND):
         pl.semaphore_signal(barrier, inc=1, device_id=(replica(d), e), device_id_type=MESH)
 
-    col = ids[...]
+    row = ids[...]
     ti = lax.broadcasted_iota(I32, (TOK, TOK), 0)
     tj = lax.broadcasted_iota(I32, (TOK, TOK), 1)
-    row = jnp.sum(jnp.where(ti == tj, col, 0), axis=0, keepdims=True)
+    col = jnp.sum(jnp.where(ti == tj, row, 0), axis=1, keepdims=True)
     slot = jnp.sum(jnp.where((col == row) & (ti < tj), 1, 0), axis=0, keepdims=True)
     kidx = ((((row >> 1) & 3) - y) & 3) * 16 + (((row >> 3) - z) & 7) * 2 + ((row & 1) ^ c)
     pos = kidx * 16 + r * CAP + slot
@@ -130,7 +130,6 @@
             remote(piece(replica(d)), mine, x_s.at[a, h], x_r.at[a, h], (replica(d), e)).start()
 
     exchange(0, 0, tokens)
-    exchange(0, 1, tokens)
 
     load_g.wait()
     gate_col = jnp.sum(jnp.where(ti == tj, gate[...], 0.0), axis=1, keepdims=True)
@@ -139,6 +138,8 @@
     def _(i):
         cols = pl.ds(pl.multiple_of(i * 512, 512), 512)
         scaled[:, cols] = (gate_col * grad_v[:, cols].astype(F32)).astype(BF16)
+
+    exchange(0, 1, tokens)
 
     pi = lax.broadcasted_iota(I32, (ROWS, MROWS), 0)
     qi = lax.broadcasted_iota(I32, (ROWS, MROWS), 1)
@@ -220,10 +221,9 @@
     def _(ch):
         select(1, 0, ch)
         select(1, 1, ch)
+
+    def send_g(ch):
         deliver(ch, lambda k: fsend.at[1, k], lambda k: frecv.at[1, k], f_s.at[1], f_r.at[2 * NC + ch], there)
-
-    for d in (2, 1, 3):
-        remote(act.at[:, r], act.at[:, r], a_s, a_r, (replica(d), e)).start()
 
     load_in.wait()
     load_out.wait()
@@ -240,7 +240,15 @@
     @pl.loop(0, NC)
     def _(ch):
         arrived(frecv.at[0, pl.ds(ch * KC, KC), 0], f_s.at[0], f_r.at[ch])
+
+    @pl.loop(0, NC)
+    def _(ch):
         arrived(frecv.at[0, pl.ds(ch * KC, KC), 1], f_s.at[0], f_r.at[NC + ch])
+
+        @pl.when(ch % 2 == 1)
+        def _():
+            send_g(ch // 2)
+
         msend[ch] = dot(compact(0, ch), win_v[...]).reshape(ND, HOME, FF)
         for d in (2, 1, 3):
             q = replica(d)
@@ -248,8 +256,13 @@
 
     def upstream(ch):
         arrived(frecv.at[1, pl.ds(ch * KC, KC)], f_s.at[1], f_r.at[2 * NC + ch])
+
+        @pl.when(ch < 2)
+        def _():
+            send_g(ch + 2)
+
         part = dot(compact(1, ch), wout_v[...]).reshape(ND, HOME, FF)
-        uown[...] = part
+        uown[ch] = part
         usend[ch] = part.astype(BF16)
         for d in (2, 1, 3):
             q = replica(d)
@@ -263,7 +276,7 @@
         def _(i):
             at = pl.ds(pl.multiple_of(i * 16, 16), 16)
             membrane = msend[ch, r, at] + mrecv[ch, 0, at] + mrecv[ch, 1, at] + mrecv[ch, 2, at]
-            up = uown[r, at]
+            up = uown[ch, r, at]
             for d in range(3):
                 up = up + urecv[ch, d, at].astype(F32)
             total = jnp.zeros_like(membrane)
@@ -287,18 +300,24 @@
                 rsend[h, pl.ds(ch * KC, KC), :, cols] = both.astype(BF16).reshape(KC, 16, PIECE)
 
     def give_back(h, ch):
-        deliver(ch, lambda k: rsend.at[h, k], lambda k: rrecv.at[h, k], r_s.at[h], r_r.at[h], back)
+        deliver(ch, lambda k: rsend.at[h, k], lambda k: rrecv.at[h, k], r_s.at[h], r_r.at[h * NC + ch], back)
 
     @pl.loop(0, NC)
     def _(ch):
         upstream(ch)
 
-        @pl.when(ch > 0)
+        @pl.when(ch >= 1)
         def _():
-            slot_grad(ch - 1)
-            give_back(0, ch - 1)
-
-        hidden(ch)
+            hidden(ch - 1)
+
+        @pl.when(ch >= 2)
+        def _():
+            slot_grad(ch - 2)
+            give_back(0, ch - 2)
+
+    hidden(NC - 1)
+    slot_grad(NC - 2)
+    give_back(0, NC - 2)
 
     def weight_grad(a, right, out):
         @pl.loop(0, 4)
@@ -308,19 +327,17 @@
 
         pltpu.make_async_copy(wg.at[a], out, w_s.at[a]).start()
 
+    for d in (2, 1, 3):
+        remote(act.at[:, r], act.at[:, r], a_s, a_r, (replica(d), e)).start()
+
+    give_back(1, 0)
     slot_grad(NC - 1)
     give_back(0, NC - 1)
 
-    @pl.loop(0, NC)
-    def _(ch):
-        give_back(1, ch)
-
-    weight_grad(0, hid, win_out)
-    arrived(act.at[:, pl.ds(0, 3)], a_s, a_r)
-    weight_grad(1, act, wout_out)
-
-    for h in range(2):
-        arrived(rrecv.at[h], r_s.at[h], r_r.at[h])
+    def returned(h, ch):
+        arrived(rrecv.at[h, pl.ds(ch * KC, KC)], r_s.at[h], r_r.at[h * NC + ch])
+
+    def combine(h):
         block = rrecv[h].reshape(NC * MROWS, MAIN)
         tsend[h, :, 0:MAIN] = dot(sel0[...], block, ((0,), (0,))).astype(BF16)
         tail = sum(dot(sel1[m], block[:, m * PIECE : (m + 1) * PIECE], ((0,), (0,))) for m in range(3))
@@ -334,6 +351,21 @@
         for d in (2, 1, 3):
             q = replica(d)
             remote(part(q), place, t_s.at[h], t_r.at[h], (q, e)).start()
+
+    returned(0, 0)
+    returned(0, 1)
+    give_back(1, 1)
+    returned(0, 2)
+    give_back(1, 2)
+    weight_grad(0, hid, win_out)
+    returned(0, 3)
+    give_back(1, 3)
+    combine(0)
+    arrived(act.at[:, pl.ds(0, 3)], a_s, a_r)
+    weight_grad(1, act, wout_out)
+    for ch in range(NC):
+        returned(1, ch)
+    combine(1)
 
     sent(pos_v.at[pl.ds(0, 3)], pos_s, pos_r)
     for a in range(2):
@@ -345,7 +377,7 @@
     sent(hid.at[pl.ds(0, 3)], h_s, h_r.at[0])
     sent(act.at[:, pl.ds(0, 3)], a_s, a_r)
     for h in range(2):
-        sent(rsend.at[h, pl.ds(1, NE - 1)], r_s.at[h], r_r.at[h])
+        sent(rsend.at[h, pl.ds(1, NE - 1)], r_s.at[h], r_r.at[h * NC])
         sent(tsend.at[h, pl.ds(0, 3 * TOK)], t_s.at[h], t_r.at[h])
     for a, out in enumerate((win_out, wout_out)):
         pltpu.make_async_copy(wg.at[a], out, w_s.at[a]).wait()
@@ -386,7 +418,7 @@
             pltpu.VMEM((2, NC * ROWS, W), BF16),
             pltpu.VMEM((NC, ND, HOME, FF), F32),
             pltpu.VMEM((NC, 3, HOME, FF), F32),
-            pltpu.VMEM((ND, HOME, FF), F32),
+            pltpu.VMEM((NC, ND, HOME, FF), F32),
             pltpu.VMEM((NC, ND, HOME, FF), BF16),
             pltpu.VMEM((NC, 3, HOME, FF), BF16),
             pltpu.VMEM((NC, ND, HOME, FF), BF16),
@@ -403,7 +435,7 @@
             dma, dma((NC,)),
             dma, dma((NC,)),
             dma, dma,
-            dma((2,)), dma((2,)),
+            dma((2,)), dma((2 * NC,)),
             dma((2,)), dma((2,)),
             dma((2,)),
         ],
@@ -412,7 +444,7 @@
         ),
         cost_estimate=pl.CostEstimate(flops=9 * 10**9, bytes_accessed=14 << 20, transcendentals=1 << 20),
     )(
-        gate_prob.reshape(1, TOK), expert_ids, threshold, tokens, grad_out,
+        gate_prob.reshape(1, TOK), expert_ids.reshape(1, TOK), threshold, tokens, grad_out,
         w_in.reshape(W, FF), w_out.reshape(W, FF), spike_counts.reshape(ROWS, FF),
     )
     return out[0], out[1][None], out[2][None]

time: 186 us -> 163 us (0.88)
  Pallas kernels: 177 us -> 156 us
    pallas_call x1, Pallas kernels: 177 us -> 156 us  [on_device(): pl.pallas_call(kernel, name='moe_backward', out_shape=(jax.ShapeDtypeStru...]
    unnamed x8 -> x7, local copies, waits for them, and re-layouts: 7.5 us -> 6.11 us
where the time goes in v2:
time: 163 us
  Pallas kernels  156 us (96%)
  local copies, waits for them, and re-layouts  6.11 us (4%)
    pallas_call x1, Pallas kernels, on_device(): pl.pallas_call(kernel, name='moe_backward', out_shape=(jax.ShapeDtypeStru...  156 us
    unnamed x7, local copies, waits for them, and re-layouts  6.11 us

profile of v2, /device:TPU:1, one launch (start us, length us, event | category | flops | bytes accessed | tf_op | source)
XLA Modules:
  0.0 162.8 jit_solution(16039534800479293668)
XLA Ops:
  0.6 156.1 %moe_backward.1 = (bf16[128,4096]{1,0:T(8,128)(2,1)}, bf16[1024,1024]{1,0:T(8,128)(2,1)}, bf16[1024,1024]{1,0:T(8,128)(2,1)}) custom-call(f32[1,128]{1,0:T(1,128)} %bitcast.12, s32[1,128]{1,0:T(1,128)} %bitcast.13, f32[1,1024]{1,0:T(1,128)} %limit.1, bf16[128,4096]{1,0:T(8,128)(2,1)} %tokens.1, bf16[128,4096]{1,0:T(8,128)(2,1)} %grads.1, ...), custom_call_target="tpu_custom_call" | custom-call | flops 8999999488 | bytes 14680064 | tf_op jit(solution)/shard_map/moe_backward/pallas_call | solution.py:392
  156.7 0.0 copy-start.1
  156.7 2.4 %copy.14 = bf16[128,4096]{1,0:T(8,128)(2,1)} copy(bf16[128,4096]{1,0:T(8,128)(2,1)} %get-tuple-element.12) | data formatting | bytes 2097152
  159.2 0.0 copy-done.1
  159.2 0.0 copy-start
  159.2 1.3 copy.15
  160.5 1.0 copy-done
  161.5 1.3 copy.16
Async XLA Ops:
  156.7 2.4 %copy-start.1 = (bf16[1024,1024]{1,0:T(8,128)(2,1)S(1)}, bf16[1024,1024]{1,0:T(8,128)(2,1)}, u32[]{:S(2)}) copy-start(bf16[1024,1024]{1,0:T(8,128)(2,1)} %get-tuple-element.7) | copy-start | bytes 6291460
  159.2 2.3 %copy-start = (bf16[1024,1024]{1,0:T(8,128)(2,1)S(1)}, bf16[1024,1024]{1,0:T(8,128)(2,1)}, u32[]{:S(2)}) copy-start(bf16[1024,1024]{1,0:T(8,128)(2,1)} %get-tuple-element.8) | copy-start | bytes 6291460

commit v3 on v2

--- a/solution.py
+++ b/solution.py
@@ -53,8 +53,8 @@
     gate, ids, limit, tokens, grads, w_in, w_out, spikes,
     tok_out, win_out, wout_out,
     grad_v, scaled, spike_v, win_v, wout_v, pos_v, xin, sel0, sel1, p0, p1, pt0, pt1,
-    fsend, frecv, rows, msend, mrecv, uown, usend, urecv, hid, act, rsend, rrecv, tsend, wg,
-    lsem, pos_s, pos_r, x_s, x_r, f_s, f_r, m_s, m_r, u_s, u_r, h_s, h_r, a_s, a_r, r_s, r_r, t_s, t_r, w_s,
+    fsend, frecv, rows, msend, mfwd, mrecv, uown, usend, urecv, hid, act, rsend, rrecv, tsend,
+    lsem, pos_s, pos_r, x_s, x_r, f_s, f_r, fw_s, fw_r, m_s, m_r, u_s, u_r, h_s, h_r, a_s, a_r, r_s, r_r, t_s, t_r,
 ):
     r = lax.axis_index("dp")
     e = lax.axis_index("expert")
@@ -228,6 +228,14 @@
     load_in.wait()
     load_out.wait()
 
+    def relay(ch):
+        arrived(mfwd.at[ch], fw_s, fw_r.at[ch])
+        for i, d in enumerate((1, 3)):
+            q = replica(d)
+            at = pl.ds(i * 24, 24)
+            msend[ch, q, at] = msend[ch, q, at] + mfwd[ch, i]
+            remote(msend.at[ch, q], mrecv.at[ch, i], m_s, m_r.at[ch], (q, e)).start()
+
     def compact(a, ch):
         at = pl.ds(pl.multiple_of(ch * ROWS, ROWS), ROWS)
         for h in range(2):
@@ -250,9 +258,16 @@
             send_g(ch // 2)
 
         msend[ch] = dot(compact(0, ch), win_v[...]).reshape(ND, HOME, FF)
-        for d in (2, 1, 3):
-            q = replica(d)
-            remote(msend.at[ch, q], mrecv.at[ch, d - 1], m_s, m_r.at[ch], (q, e)).start()
+        far = replica(2)
+        for i, d in enumerate((1, 3)):
+            part = msend.at[ch, far, pl.ds(i * 24, 24)]
+            remote(part, mfwd.at[ch, i], fw_s, fw_r.at[ch], (replica(d), e)).start()
+
+        @pl.when(ch >= 1)
+        def _():
+            relay(ch - 1)
+
+    relay(NC - 1)
 
     def upstream(ch):
         arrived(frecv.at[1, pl.ds(ch * KC, KC)], f_s.at[1], f_r.at[2 * NC + ch])
@@ -275,7 +290,7 @@
         @pl.loop(0, 3)
         def _(i):
             at = pl.ds(pl.multiple_of(i * 16, 16), 16)
-            membrane = msend[ch, r, at] + mrecv[ch, 0, at] + mrecv[ch, 1, at] + mrecv[ch, 2, at]
+            membrane = msend[ch, r, at] + mrecv[ch, 0, at] + mrecv[ch, 1, at]
             up = uown[ch, r, at]
             for d in range(3):
                 up = up + urecv[ch, d, at].astype(F32)
@@ -323,9 +338,8 @@
         @pl.loop(0, 4)
         def _(i):
             at = pl.ds(pl.multiple_of(i * 256, 256), 256)
-            wg[a, at, :] = dot(rows[a, :, at], right[...].reshape(NC * ROWS, FF), ((0,), (0,))).astype(BF16)
-
-        pltpu.make_async_copy(wg.at[a], out, w_s.at[a]).start()
+            out[at, :] = dot(rows[a, :, at], right[...].reshape(NC * ROWS, FF), ((0,), (0,))).astype(BF16)
+
 
     for d in (2, 1, 3):
         remote(act.at[:, r], act.at[:, r], a_s, a_r, (replica(d), e)).start()
@@ -372,15 +386,14 @@
         for h in range(2):
             sent(xin.at[a, pl.ds(0, 3 * TOK), pl.ds(h * HALF, HALF)], x_s.at[a, h], x_r.at[a, h])
         sent(fsend.at[a, pl.ds(1, NE - 1)], f_s.at[a], f_r.at[0])
-    sent(msend.at[pl.ds(0, 3)], m_s, m_r.at[0])
+    sent(msend.at[pl.ds(0, 2)], m_s, m_r.at[0])
+    sent(msend.at[0], fw_s, fw_r.at[0])
     sent(usend.at[pl.ds(0, 3)], u_s, u_r.at[0])
     sent(hid.at[pl.ds(0, 3)], h_s, h_r.at[0])
     sent(act.at[:, pl.ds(0, 3)], a_s, a_r)
     for h in range(2):
         sent(rsend.at[h, pl.ds(1, NE - 1)], r_s.at[h], r_r.at[h * NC])
         sent(tsend.at[h, pl.ds(0, 3 * TOK)], t_s.at[h], t_r.at[h])
-    for a, out in enumerate((win_out, wout_out)):
-        pltpu.make_async_copy(wg.at[a], out, w_s.at[a]).wait()
     for h in range(2):
         arrived(tok_out.at[:, pl.ds(0, ND * HALF)], t_s.at[h], t_r.at[h])
 
@@ -393,12 +406,12 @@
         kernel,
         name="moe_backward",
         out_shape=(
-            jax.ShapeDtypeStruct((TOK, ND * W), BF16),
-            jax.ShapeDtypeStruct((W, FF), BF16),
-            jax.ShapeDtypeStruct((W, FF), BF16),
+            pltpu.VMEM((TOK, ND * W), BF16),
+            pltpu.VMEM((W, FF), BF16),
+            pltpu.VMEM((W, FF), BF16),
         ),
         in_specs=[vmem, vmem, vmem] + [hbm] * 5,
-        out_specs=(hbm, hbm, hbm),
+        out_specs=(vmem, vmem, vmem),
         scratch_shapes=[
             pltpu.VMEM((TOK, ND * W), BF16),
             pltpu.VMEM((TOK, ND * W), BF16),
@@ -417,7 +430,8 @@
             pltpu.VMEM((2, NE, 2, 16, MAIN), BF16),
             pltpu.VMEM((2, NC * ROWS, W), BF16),
             pltpu.VMEM((NC, ND, HOME, FF), F32),
-            pltpu.VMEM((NC, 3, HOME, FF), F32),
+            pltpu.VMEM((NC, 2, 24, FF), F32),
+            pltpu.VMEM((NC, 2, HOME, FF), F32),
             pltpu.VMEM((NC, ND, HOME, FF), F32),
             pltpu.VMEM((NC, ND, HOME, FF), BF16),
             pltpu.VMEM((NC, 3, HOME, FF), BF16),
@@ -426,7 +440,6 @@
             pltpu.VMEM((2, NE, 16, MAIN), BF16),
             pltpu.VMEM((2, NE, 16, MAIN), BF16),
             pltpu.VMEM((2, ND * TOK, HALF), BF16),
-            pltpu.VMEM((2, W, FF), BF16),
             dma((4,)),
             dma, dma,
             dma((2, 2)), dma((2, 2)),
@@ -434,13 +447,13 @@
             dma, dma((NC,)),
             dma, dma((NC,)),
             dma, dma((NC,)),
+            dma, dma((NC,)),
             dma, dma,
             dma((2,)), dma((2 * NC,)),
             dma((2,)), dma((2,)),
-            dma((2,)),
         ],
         compiler_params=pltpu.CompilerParams(
-            collective_id=0, has_side_effects=True, vmem_limit_bytes=58 << 20
+            collective_id=0, has_side_effects=True, vmem_limit_bytes=52 << 20
         ),
         cost_estimate=pl.CostEstimate(flops=9 * 10**9, bytes_accessed=14 << 20, transcendentals=1 << 20),
     )(

time: 163 us -> 155 us (0.951)
  Pallas kernels: 156 us -> 150 us
  local copies, waits for them, and re-layouts: 6.11 us -> 3.61 us
    pallas_call x1, Pallas kernels: 156 us -> 150 us  [on_device(): pl.pallas_call(kernel, name='moe_backward', out_shape=(pltpu.VMEM((TOK, N...]
    unnamed x7 -> x3, local copies, waits for them, and re-layouts: 6.11 us -> 3.61 us
where the time goes in v3:
time: 155 us
  Pallas kernels  150 us (97%)
  local copies, waits for them, and re-layouts  3.61 us (2%)
    pallas_call x1, Pallas kernels, on_device(): pl.pallas_call(kernel, name='moe_backward', out_shape=(pltpu.VMEM((TOK, N...  150 us
    unnamed x3, local copies, waits for them, and re-layouts  3.61 us

profile of v3, /device:TPU:1, one launch (start us, length us, event | category | flops | bytes accessed | tf_op | source)
XLA Modules:
  0.0 154.7 jit_solution(3412325007943633605)
XLA Ops:
  0.6 150.5 %moe_backward.1 = (bf16[128,4096]{1,0:T(8,128)(2,1)S(1)}, bf16[1024,1024]{1,0:T(8,128)(2,1)S(1)}, bf16[1024,1024]{1,0:T(8,128)(2,1)S(1)}) custom-call(f32[1,128]{1,0:T(1,128)} %bitcast.12, s32[1,128]{1,0:T(1,128)} %bitcast.13, f32[1,1024]{1,0:T(1,128)} %limit.1, bf16[128,4096]{1,0:T(8,128)(2,1)} %tokens.1, bf16[128,4096]{1,0:T(8,128)(2,1)} %grads.1, ...), custom_call_target="tpu_custom_call" | custom-call | flops 8999999488 | bytes 14680064 | tf_op jit(solution)/shard_map/moe_backward/pallas_call | solution.py:405
  151.1 1.0 copy.14
  152.1 1.3 copy.15
  153.4 1.3 copy.16

commit v4 on v3

--- a/solution.py
+++ b/solution.py
@@ -341,12 +341,12 @@
             out[at, :] = dot(rows[a, :, at], right[...].reshape(NC * ROWS, FF), ((0,), (0,))).astype(BF16)
 
 
-    for d in (2, 1, 3):
-        remote(act.at[:, r], act.at[:, r], a_s, a_r, (replica(d), e)).start()
-
     give_back(1, 0)
     slot_grad(NC - 1)
     give_back(0, NC - 1)
+
+    for d in (2, 1, 3):
+        remote(act.at[:, r], act.at[:, r], a_s, a_r, (replica(d), e)).start()
 
     def returned(h, ch):
         arrived(rrecv.at[h, pl.ds(ch * KC, KC)], r_s.at[h], r_r.at[h * NC + ch])

time: 155 us -> 155 us (level)
  no operation moved by 1% of the time
where the time goes in v4:
time: 155 us
  Pallas kernels  150 us (97%)
  local copies, waits for them, and re-layouts  3.61 us (2%)
    pallas_call x1, Pallas kernels, on_device(): pl.pallas_call(kernel, name='moe_backward', out_shape=(pltpu.VMEM((TOK, N...  150 us
    unnamed x3, local copies, waits for them, and re-layouts  3.61 us

profile of v4, /device:TPU:1, one launch (start us, length us, event | category | flops | bytes accessed | tf_op | source)
XLA Modules:
  0.0 154.7 jit_solution(435408097618184299)
XLA Ops:
  0.6 150.5 %moe_backward.1 = (bf16[128,4096]{1,0:T(8,128)(2,1)S(1)}, bf16[1024,1024]{1,0:T(8,128)(2,1)S(1)}, bf16[1024,1024]{1,0:T(8,128)(2,1)S(1)}) custom-call(f32[1,128]{1,0:T(1,128)} %bitcast.12, s32[1,128]{1,0:T(1,128)} %bitcast.13, f32[1,1024]{1,0:T(1,128)} %limit.1, bf16[128,4096]{1,0:T(8,128)(2,1)} %tokens.1, bf16[128,4096]{1,0:T(8,128)(2,1)} %grads.1, ...), custom_call_target="tpu_custom_call" | custom-call | flops 8999999488 | bytes 14680064 | tf_op jit(solution)/shard_map/moe_backward/pallas_call | solution.py:405
  151.1 1.0 copy.14
  152.1 1.3 copy.15
  153.4 1.3 copy.16
